TPU v7x, 32 devices: a whole 2x2x4 slice. The times are simulated.
32 devices in a mesh: sta: 16 (over z, x, core), band: 2 (over y).
Axes of the slice: x: 2, y: 2, z: 4, core: 2. Of those that a mesh axis runs over, the one named last changes fastest.
Arguments:
- spectra: bfloat16 [2, 8, 6144, 1024], P(None, None, 'sta', 'band')
- half_width: int32 [1024], P('band'), may hold values from 1 to 8, as said below
Outputs:
- correlations: bfloat16 [6144, 3, 8, 384], P('sta', None, 'band')
Inputs may be any that keep to these rules, and one draw needn't show every extreme that they name: `half_width`: at most 8, and exactly 8 at one bin or more.
All inputs are finite; a program needn't handle non-finite values.
Results may differ from a plain program's by a relative error of at most 0.0062.
Values may be sent and summed in bfloat16 or wider, within the bound.
A program may use at most 192 MiB of HBM per device.

v0:
```python
import math

import jax
import jax.numpy as jnp
from jax import lax
from jax.sharding import PartitionSpec as P

NF = 1024
ROUNDS = 3
LAGS = 4
LAG_STEP = 8
WMAX = 8


def padded_2(cells, sides, width):
    for axis, dim in sides:
        count = lax.axis_size(axis)
        ends = count - 1
        head = lax.slice_in_dim(cells, 0, width, axis=dim)
        tail = lax.slice_in_dim(cells, cells.shape[dim] - width, cells.shape[dim], axis=dim)
        cells = jnp.concatenate(
            [
                lax.ppermute(tail, axis, [(i, (i + 1) % count) for i in range(ends)]),
                cells,
                lax.ppermute(head, axis, [((i + 1) % count, i) for i in range(ends)]),
            ],
            axis=dim,
        )
    return cells


def from_behind(value, axis, steps):
    count = lax.axis_size(axis)
    pairs = [(source, (source + steps) % count) for source in range(count)]
    return lax.ppermute(value, axis, pairs)


def rotate_part(part, cosines, sines):
    real_part = part[0].astype(jnp.float32)[None]
    imag_part = part[1].astype(jnp.float32)[None]
    cos_block = cosines[:, None, None, :]
    sin_block = sines[:, None, None, :]
    rot_real = (real_part * cos_block - imag_part * sin_block).astype(jnp.bfloat16)
    rot_imag = (real_part * sin_block + imag_part * cos_block).astype(jnp.bfloat16)
    return jnp.stack([rot_real, rot_imag])


def correlate(left_part, rotated, norm_factor):
    summed = jnp.einsum("cspf,clsqf->plq", left_part, rotated, preferred_element_type=jnp.float32)
    return (summed * norm_factor).astype(jnp.bfloat16)


def shards(spectra, half_width):
    segs = spectra.shape[1]
    chans = spectra.shape[2]
    bins = spectra.shape[3]
    stations = chans // 3
    energy = jnp.sum(jnp.square(spectra.astype(jnp.float32)), axis=(0, 1))
    energy = jnp.sum(energy.reshape(stations, 3, bins), axis=1)
    padded = padded_2(energy, (("band", 1),), WMAX)
    rim_width = (padded.shape[1] - bins) // 2
    first_bin = lax.axis_index("band") * bins
    inner = first_bin + jnp.arange(bins, dtype=jnp.int32)
    outer = first_bin - rim_width + jnp.arange(bins + 2 * rim_width, dtype=jnp.int32)
    window = (jnp.abs(outer[:, None] - inner[None, :]) <= half_width[None, :]).astype(jnp.float32)
    inside = ((outer >= 0) & (outer < NF)).astype(jnp.float32)
    window_sum = jnp.dot(padded, window, precision=lax.Precision.HIGHEST)
    counts = jnp.dot(inside, window, precision=lax.Precision.HIGHEST)
    amplitude = jnp.sqrt(window_sum / (3.0 * segs * counts) + 1e-06)
    whitened = (spectra.astype(jnp.float32) / jnp.repeat(amplitude, 3, axis=0)[None, None]).astype(
        jnp.bfloat16
    )
    lag_values = jnp.arange(LAGS, dtype=jnp.float32) * LAG_STEP
    phases = math.pi * lag_values[:, None] * inner.astype(jnp.float32)[None, :] / NF
    cosines = jnp.cos(phases)
    sines = jnp.sin(phases)
    norm_factor = 1.0 / math.sqrt(segs * bins)
    results = []
    for offset in range(1, ROUNDS + 1):
        partner = from_behind(whitened, "sta", offset)
        results.append(correlate(whitened, rotate_part(partner, cosines, sines), norm_factor))
    return jnp.stack(results, axis=1)


def solution(mesh):
    in_specs = (P(None, None, "sta", "band"), P("band"))
    out_specs = P("sta", None, "band", None)
    return jax.shard_map(shards, mesh=mesh, in_specs=in_specs, out_specs=out_specs, check_vma=False)
```

profile of v0, /device:TPU:0, one launch (start us, length us, event | category | flops | bytes accessed | tf_op | source)
XLA Modules:
  0.0 468.3 jit_solution(4308722860892720508)
XLA Ops:
  0.0 0.0 copy-start.1
  0.0 4.1 fusion.12
  4.1 0.3 reshape.142
  4.4 0.6 reduce_sum.19
  5.1 0.1 fusion.74
  5.2 4.9 %collective-permute-start = (f32[128,8]{1,0:T(8,128)S(1)}, f32[128,8]{1,0:T(8,128)S(1)}, u32[]{:S(2)}, u32[]{:S(2)}) collective-permute-start(f32[128,8]{1,0:T(8,128)S(1)} %get-tuple-element.17), channel_id=1, source_target_pairs={{0,1},{2,3},{4,5},{6,7},{8,9},{10,11},{12,13},{14,15},{16,17},{18,... | collective-permute-start | bytes 12296 | tf_op jit(solution)/shard_map/ppermute | solution.py:23
  10.0 1.3 collective-permute-start.1
  11.4 0.0 copy-done.1
  11.4 0.5 fusion.55
  11.9 0.0 collective-permute-done
  11.9 4.3 collective-permute-done.1
  16.2 0.9 fusion.54
  17.1 0.2 broadcast_in_dim.2
  17.3 0.4 div.26
  17.7 4.3 fusion.13
  22.0 0.0 copy-start
  22.0 0.1 collective-permute-start.4
  22.0 1.5 collective-permute-start.3
  23.6 1.3 collective-permute-start.2
  24.9 0.1 fusion.68
  25.1 130.6 %collective-permute-done.4 = bf16[2,8,384,512]{3,2,1,0:T(8,128)(2,1)} collective-permute-done((bf16[2,8,384,512]{3,2,1,0:T(8,128)(2,1)S(1)}, bf16[2,8,384,512]{3,2,1,0:T(8,128)(2,1)}, u32[]{:S(2)}, u32[]{:S(2)}) %collective-permute-start.4) | collective-permute-done | bytes 6291488 | tf_op jit(solution)/shard_map/ppermute | solution.py:35
  155.7 6.5 %fusion.18 = (f32[8,384,512]{2,1,0:T(8,128)S(1)}, f32[8,384,512]{2,1,0:T(8,128)}) fusion(bf16[2,8,384,512]{3,2,1,0:T(8,128)(2,1)} %collective-permute-done.4), kind=kLoop, calls=%fused_computation.29 | loop fusion | flops 3145728 | bytes 18874368 | tf_op jit(solution)/shard_map/mul | solution.py:43
  162.2 0.0 copy-done
  162.2 135.6 %collective-permute-done.3 = bf16[2,8,384,512]{3,2,1,0:T(8,128)(2,1)} collective-permute-done((bf16[2,8,384,512]{3,2,1,0:T(8,128)(2,1)S(1)}, bf16[2,8,384,512]{3,2,1,0:T(8,128)(2,1)}, u32[]{:S(2)}, u32[]{:S(2)}) %collective-permute-start.3) | collective-permute-done | bytes 6291488 | tf_op jit(solution)/shard_map/ppermute | solution.py:35
  297.8 9.1 %fusion.20 = (f32[8,384,512]{2,1,0:T(8,128)}, f32[8,384,512]{2,1,0:T(8,128)}) fusion(bf16[2,8,384,512]{3,2,1,0:T(8,128)(2,1)} %collective-permute-done.3), kind=kLoop, calls=%fused_computation.33 | loop fusion | flops 3145728 | bytes 18874368 | tf_op jit(solution)/shard_map/mul | solution.py:43
  306.9 58.0 %collective-permute-done.2 = bf16[2,8,384,512]{3,2,1,0:T(8,128)(2,1)} collective-permute-done((bf16[2,8,384,512]{3,2,1,0:T(8,128)(2,1)S(1)}, bf16[2,8,384,512]{3,2,1,0:T(8,128)(2,1)}, u32[]{:S(2)}, u32[]{:S(2)}) %collective-permute-start.2) | collective-permute-done | bytes 6291488 | tf_op jit(solution)/shard_map/ppermute | solution.py:35
  364.9 9.1 %fusion.22 = (f32[8,384,512]{2,1,0:T(8,128)}, f32[8,384,512]{2,1,0:T(8,128)}) fusion(bf16[2,8,384,512]{3,2,1,0:T(8,128)(2,1)} %collective-permute-done.2), kind=kLoop, calls=%fused_computation.37 | loop fusion | flops 3145728 | bytes 18874368 | tf_op jit(solution)/shard_map/mul | solution.py:43
  374.0 39.3 %subtract_convert_fusion.2 = (bf16[1,4,8,384,512]{4,3,2,0,1:T(8,128)(2,1)}, bf16[1,4,8,384,512]{4,3,2,0,1:T(8,128)(2,1)}, bf16[1,4,8,384,512]{4,3,2,0,1:T(8,128)...) fusion(f32[4,512]{1,0:T(4,128)S(1)} %get-tuple-element.24, ...), kind=kLoop, calls=%fused_computation.17 | loop fusion | flops 150994944 | bytes 113262592 | tf_op jit(solution)/shard_map/convert_element_type | solution.py:43
  413.3 16.6 %fusion.38 = bf16[384,1,4,384]{3,0,2,1:T(8,128)(2,1)S(1)} fusion(bf16[1,4,8,384,512]{4,3,2,0,1:T(8,128)(2,1)} %get-tuple-element.6, bf16[1,4,8,384,512]{4,3,2,0,1:T(8,128)(2,1)} %get-tuple-element.5, bf16[2,8,384,512]{3,2,1,0:T(8,128)(2,1)} %copy-done), kind=kOutput, calls=%fused_computation.44 | convolution fusion | flops 9715187712 | bytes 32636928 | tf_op jit(solution)/shard_map/cspf,clsqf->plq/dot_general | solution.py:49
  429.8 16.6 %fusion.43 = bf16[384,1,4,384]{3,0,2,1:T(8,128)(2,1)S(1)} fusion(bf16[1,4,8,384,512]{4,3,2,0,1:T(8,128)(2,1)} %get-tuple-element.19, bf16[1,4,8,384,512]{4,3,2,0,1:T(8,128)(2,1)} %get-tuple-element.20, bf16[2,8,384,512]{3,2,1,0:T(8,128)(2,1)} %copy-done), kind=kOutput, calls=%fused_computation.45 | convolution fusion | flops 9715187712 | bytes 32636928 | tf_op jit(solution)/shard_map/cspf,clsqf->plq/dot_general | solution.py:49
  446.4 16.8 %fusion.48 = bf16[384,1,4,384]{3,0,2,1:T(8,128)(2,1)S(1)} fusion(bf16[1,4,8,384,512]{4,3,2,0,1:T(8,128)(2,1)} %get-tuple-element.21, bf16[1,4,8,384,512]{4,3,2,0,1:T(8,128)(2,1)} %get-tuple-element.22, bf16[2,8,384,512]{3,2,1,0:T(8,128)(2,1)} %copy-done), kind=kOutput, calls=%fused_computation.46 | convolution fusion | flops 9715187712 | bytes 32636928 | tf_op jit(solution)/shard_map/cspf,clsqf->plq/dot_general | solution.py:49
  463.2 0.5 pad_maximum_fusion
  463.7 4.5 copy.4
  (7 shorter events, 0.0 us)
Async XLA Ops:
  0.0 11.4 %copy-start.1 = (s32[512]{0:T(512)S(1)}, s32[512]{0:T(512)}, u32[]{:S(2)}) copy-start(s32[512]{0:T(512)} %param.3) | copy-start | bytes 6148
  5.2 6.8 %collective-permute-start = (f32[128,8]{1,0:T(8,128)S(1)}, f32[128,8]{1,0:T(8,128)S(1)}, u32[]{:S(2)}, u32[]{:S(2)}) collective-permute-start(f32[128,8]{1,0:T(8,128)S(1)} %get-tuple-element.17), channel_id=1, source_target_pairs={{0,1},{2,3},{4,5},{6,7},{8,9},{10,11},{12,13},{14,15},{16,17},{18,... | collective-permute-start | bytes 12296 | tf_op jit(solution)/shard_map/ppermute | solution.py:23
  10.0 6.2 %collective-permute-start.1 = (f32[128,8]{1,0:T(8,128)S(1)}, f32[128,8]{1,0:T(8,128)S(1)}, u32[]{:S(2)}, u32[]{:S(2)}) collective-permute-start(f32[128,8]{1,0:T(8,128)S(1)} %get-tuple-element.18), channel_id=1, source_target_pairs={{1,0},{3,2},{5,4},{7,6},{9,8},{11,10},{13,12},{15,14},{17,16},{19,... | collective-permute-start | bytes 12296 | tf_op jit(solution)/shard_map/ppermute | solution.py:25
  22.0 140.2 %copy-start = (bf16[2,8,384,512]{3,2,1,0:T(8,128)(2,1)}, bf16[2,8,384,512]{3,2,1,0:T(8,128)(2,1)S(1)}, u32[]{:S(2)}) copy-start(bf16[2,8,384,512]{3,2,1,0:T(8,128)(2,1)S(1)} %fusion.13) | copy-start | bytes 18874372
  22.0 133.7 %collective-permute-start.4 = (bf16[2,8,384,512]{3,2,1,0:T(8,128)(2,1)S(1)}, bf16[2,8,384,512]{3,2,1,0:T(8,128)(2,1)}, u32[]{:S(2)}, u32[]{:S(2)}) collective-permute-start(bf16[2,8,384,512]{3,2,1,0:T(8,128)(2,1)S(1)} %fusion.13), channel_id=1, source_target_pairs={{0,6},{2,8},{4,10},{6,12},{8,14},{10,16},{12,18},{14,20},{16,22},{... | collective-permute-start | bytes 18874376 | tf_op jit(solution)/shard_map/ppermute | solution.py:35
  22.0 275.7 %collective-permute-start.3 = (bf16[2,8,384,512]{3,2,1,0:T(8,128)(2,1)S(1)}, bf16[2,8,384,512]{3,2,1,0:T(8,128)(2,1)}, u32[]{:S(2)}, u32[]{:S(2)}) collective-permute-start(bf16[2,8,384,512]{3,2,1,0:T(8,128)(2,1)S(1)} %fusion.13), channel_id=1, source_target_pairs={{0,4},{2,6},{4,8},{6,10},{8,12},{10,14},{12,16},{14,18},{16,20},{1... | collective-permute-start | bytes 18874376 | tf_op jit(solution)/shard_map/ppermute | solution.py:35
  23.6 341.3 %collective-permute-start.2 = (bf16[2,8,384,512]{3,2,1,0:T(8,128)(2,1)S(1)}, bf16[2,8,384,512]{3,2,1,0:T(8,128)(2,1)}, u32[]{:S(2)}, u32[]{:S(2)}) collective-permute-start(bf16[2,8,384,512]{3,2,1,0:T(8,128)(2,1)S(1)} %fusion.13), channel_id=1, source_target_pairs={{0,2},{2,4},{4,6},{6,8},{8,10},{10,12},{12,14},{14,16},{16,18},{18... | collective-permute-start | bytes 18874376 | tf_op jit(solution)/shard_map/ppermute | solution.py:35
where the time goes:
time: 468 us
  waiting for transfers between devices  328 us (70%)
  other arithmetic  73.7 us (16%)
  matrix products  51.3 us (11%)
  starting transfers between devices  9.11 us (2%)
  local copies, waits for them, and re-layouts  5.54 us (1%)
    ppermute x3, waiting for transfers between devices, from_behind(): return lax.ppermute(value, axis, pairs)  324 us
    dot_general x3, matrix products, correlate(): jnp.einsum('cspf,clsqf->plq', left_part, rotated, preferred_element_type=...  49.9 us
    convert_element_type x1, other arithmetic, rotate_part(): (real_part * cos_block - imag_part * sin_block).astype(jnp.bfloat16)  39.3 us
    mul x3, other arithmetic, rotate_part(): real_part * cos_block - imag_part * sin_block  24.7 us
  transfers between devices with their start and end apart: 5, of which 4 were waited for; matrix products, arithmetic and copies ran while one was open for 3% of the time, Pallas kernels for 0%

commit v1 on v0

v1 whole, which is shorter than its diff:
```python
import functools
import math

import jax
import jax.numpy as jnp
from jax import lax
from jax.experimental import pallas as pl
from jax.experimental.pallas import tpu as pltpu
from jax.sharding import PartitionSpec as P

ROUNDS = 3
LAGS = 4
LAG_STEP = 8
WMAX = 8
LANES = 128
ROWS = 32
EARLY = 2
MESH = pl.DeviceIdType.MESH
HIGHEST = lax.Precision.HIGHEST
F32 = jnp.float32
BF16 = jnp.bfloat16


def kernel(
    groups, bands, spectra, half_width, cosines, sines, out,
    rot, got, acc, amps, scale, energy, padded,
    load_sem, send_sem, recv_sem, edge_send, edge_recv,
):
    _, segs, chans, bins = spectra.shape
    stations = chans // 3
    me = lax.axis_index("sta")
    band = lax.axis_index("band")
    core = lax.rem(me, 2)
    odd = lax.rem(me // 2, 2)
    first = core == 0
    second = core == 1
    direct = jnp.logical_or(odd == 0, first)
    relays = jnp.logical_and(odd == 1, first)

    def at(step):
        return {"sta": lax.rem(me + step + groups, groups)}

    right = {"band": lax.rem(band + 1, bands)}
    left = {"band": lax.rem(band + bands - 1, bands)}

    barrier = pltpu.get_barrier_semaphore()
    peers = [at(step) for step in (-3, -2, -1, 1, 2, 3)] + [left, right]
    for peer in peers:
        pl.semaphore_signal(barrier, inc=1, device_id=peer, device_id_type=MESH)
    pl.semaphore_wait(barrier, len(peers))

    def copy(flow, slot, step, s, source):
        last = isinstance(s, int) and s == segs
        target = amps.at[slot] if last else got.at[slot, s]
        if source is None:
            origin = amps.at[ROUNDS] if last else spectra.at[:, s]
        else:
            origin = amps.at[source] if last else got.at[source, s]
        return pltpu.make_async_remote_copy(
            src_ref=origin, dst_ref=target,
            send_sem=send_sem.at[flow, s], recv_sem=recv_sem.at[slot, s],
            device_id=at(step), device_id_type=MESH,
        )

    own_flows = [
        (direct, lambda s: copy(0, 1, 2, s, None)),
        (second, lambda s: copy(1, 2, 3, s, None)),
        (first, lambda s: copy(2, 0, 1, s, None)),
    ]
    relay = (relays, lambda s: copy(3, 1, -1, s, 2))
    swaps = [
        (first, lambda s: copy(4, 2, 1, s, 1)),
        (second, lambda s: copy(4, 0, -1, s, 1)),
    ]

    def start(flows, s):
        for cond, make in flows:
            @pl.when(cond)
            def _():
                make(s).start()

    def arrived(slot, s):
        copy(0, slot, 2, s, None).wait_recv()

    def forward(s):
        @pl.when(relays)
        def _():
            arrived(2, s)
            relay[1](s).start()

    def arrived_third(s):
        @pl.when(jnp.logical_not(relays))
        def _():
            arrived(2, s)

    def load(s):
        return pltpu.make_async_copy(spectra.at[:, s], rot.at[s, :, 0], load_sem.at[s])

    @pl.loop(0, segs)
    def _(s):
        load(s).start()

    @pl.loop(0, EARLY)
    def _(s):
        start(own_flows, s)

    @pl.loop(0, segs)
    def _(s):
        load(s).wait()

    @pl.loop(0, chans // ROWS)
    def _(i):
        rows = pl.ds(pl.multiple_of(i * ROWS, ROWS), ROWS)
        total = jnp.zeros((ROWS, bins), F32)
        for s in range(segs):
            for c in range(2):
                part = rot[s, c, 0, rows, :].astype(F32)
                total = total + part * part
        energy[rows, :] = total

    member = (
        lax.broadcasted_iota(jnp.int32, (stations, chans), 1) // 3
        == lax.broadcasted_iota(jnp.int32, (stations, chans), 0)
    ).astype(F32)
    spread = (
        lax.broadcasted_iota(jnp.int32, (chans, stations), 0) // 3
        == lax.broadcasted_iota(jnp.int32, (chans, stations), 1)
    ).astype(F32)
    padded[:, LANES:LANES + bins] = jnp.dot(
        member, energy[...], precision=HIGHEST, preferred_element_type=F32
    )
    to_right = pltpu.make_async_remote_copy(
        src_ref=padded.at[:, pl.ds(bins, LANES)], dst_ref=padded.at[:, pl.ds(0, LANES)],
        send_sem=edge_send.at[0], recv_sem=edge_recv.at[0],
        device_id=right, device_id_type=MESH,
    )
    to_left = pltpu.make_async_remote_copy(
        src_ref=padded.at[:, pl.ds(LANES, LANES)],
        dst_ref=padded.at[:, pl.ds(LANES + bins, LANES)],
        send_sem=edge_send.at[1], recv_sem=edge_recv.at[1],
        device_id=left, device_id_type=MESH,
    )
    to_right.start()
    to_left.start()
    to_right.wait()
    to_left.wait()

    width = half_width[...]
    place = band * bins + lax.broadcasted_iota(jnp.int32, (1, bins), 1)
    window_sum = jnp.zeros((stations, bins), F32)
    counts = jnp.zeros((1, bins), F32)
    for d in range(-WMAX, WMAX + 1):
        other = place + d
        inside = (abs(d) <= width) & (other >= 0) & (other < bands * bins)
        weight = inside.astype(F32)
        window_sum = window_sum + jnp.where(
            jnp.broadcast_to(weight, (stations, bins)) > 0.0,
            padded[:, LANES + d:LANES + d + bins], 0.0,
        )
        counts = counts + weight
    amps[ROUNDS] = 1.0 / jnp.sqrt(window_sum / (3.0 * segs * counts) + 1e-06)

    start(own_flows, segs)

    @pl.loop(EARLY, segs)
    def _(s):
        start(own_flows, s)

    def expand(slot):
        scale[slot] = jnp.dot(
            spread, amps[slot], precision=HIGHEST, preferred_element_type=F32
        )

    expand(ROUNDS)

    @pl.loop(0, segs)
    def _(s):
        @pl.loop(0, chans // ROWS)
        def _(i):
            rows = pl.ds(pl.multiple_of(i * ROWS, ROWS), ROWS)
            factor = scale[ROUNDS, rows, :]
            real = (rot[s, 0, 0, rows, :].astype(F32) * factor).astype(BF16)
            imag = (rot[s, 1, 0, rows, :].astype(F32) * factor).astype(BF16)
            rot[s, 0, 0, rows, :] = real
            rot[s, 1, 0, rows, :] = imag
            real = real.astype(F32)
            imag = imag.astype(F32)
            for lag in range(1, LAGS):
                cosine = cosines[lag:lag + 1, :]
                sine = sines[lag:lag + 1, :]
                rot[s, 0, lag, rows, :] = (real * cosine + imag * sine).astype(BF16)
                rot[s, 1, lag, rows, :] = (imag * cosine - real * sine).astype(BF16)

    forward(segs)
    forward(0)
    arrived(1, segs)
    start(swaps, segs)
    acc[...] = jnp.zeros_like(acc)
    expand(1)
    arrived_third(segs)
    expand(2)
    arrived(0, segs)
    expand(0)

    def add(slot, s):
        for c in range(2):
            other = (got[slot, s, c].astype(F32) * scale[slot]).astype(BF16)
            mine = rot[s, c].reshape(LAGS * chans, bins)
            acc[slot] += lax.dot_general(
                mine, other, (((1,), (1,)), ((), ())), preferred_element_type=F32
            )

    @pl.loop(0, segs)
    def _(s):
        @pl.when(s + 1 < segs)
        def _():
            forward(s + 1)

        arrived(1, s)
        start(swaps, s)
        add(1, s)
        arrived_third(s)
        add(2, s)
        arrived(0, s)
        add(0, s)

    norm = 1.0 / math.sqrt(segs * bins)
    for slot in range(ROUNDS):
        @pl.loop(0, LAGS * chans // ROWS)
        def _(i):
            rows = pl.ds(pl.multiple_of(i * ROWS, ROWS), ROWS)
            out[slot, rows, :] = (acc[slot, rows, :] * norm).astype(BF16)

    def sent(s):
        for cond, make in own_flows + [relay] + swaps:
            @pl.when(cond)
            def _():
                make(s).wait_send()

    @pl.loop(0, segs)
    def _(s):
        sent(s)

    sent(segs)


def shards(groups, bands, spectra, half_width):
    _, segs, chans, bins = spectra.shape
    inner = lax.axis_index("band") * bins + jnp.arange(bins, dtype=jnp.int32)
    lag_values = jnp.arange(LAGS, dtype=F32) * LAG_STEP
    phases = math.pi * lag_values[:, None] * inner.astype(F32)[None, :] / (bands * bins)
    vmem = pl.BlockSpec(memory_space=pltpu.VMEM)
    pieces = segs + 1
    out = pl.pallas_call(
        functools.partial(kernel, groups, bands),
        out_shape=jax.ShapeDtypeStruct((ROUNDS, LAGS * chans, chans), BF16),
        in_specs=[pl.BlockSpec(memory_space=pl.ANY), vmem, vmem, vmem],
        out_specs=vmem,
        scratch_shapes=[
            pltpu.VMEM((segs, 2, LAGS, chans, bins), BF16),
            pltpu.VMEM((ROUNDS, segs, 2, chans, bins), BF16),
            pltpu.VMEM((ROUNDS, LAGS * chans, chans), F32),
            pltpu.VMEM((ROUNDS + 1, chans // 3, bins), F32),
            pltpu.VMEM((ROUNDS + 1, chans, bins), F32),
            pltpu.VMEM((chans, bins), F32),
            pltpu.VMEM((chans // 3, bins + 2 * LANES), F32),
            pltpu.SemaphoreType.DMA((segs,)),
            pltpu.SemaphoreType.DMA((5, pieces)),
            pltpu.SemaphoreType.DMA((ROUNDS, pieces)),
            pltpu.SemaphoreType.DMA((2,)),
            pltpu.SemaphoreType.DMA((2,)),
        ],
        compiler_params=pltpu.CompilerParams(
            collective_id=0, has_side_effects=True, vmem_limit_bytes=66_500_000
        ),
        cost_estimate=pl.CostEstimate(
            flops=2 * ROUNDS * LAGS * chans * chans * 2 * segs * bins,
            bytes_accessed=2 * spectra.size * 4, transcendentals=0,
        ),
    )(spectra, half_width.reshape(1, bins), jnp.cos(phases), jnp.sin(phases))
    return jnp.transpose(out.reshape(ROUNDS, LAGS, chans, chans), (2, 0, 1, 3))


def solution(mesh):
    in_specs = (P(None, None, "sta", "band"), P("band"))
    out_specs = P("sta", None, "band", None)
    body = functools.partial(shards, mesh.shape["sta"], mesh.shape["band"])
    return jax.shard_map(body, mesh=mesh, in_specs=in_specs, out_specs=out_specs, check_vma=False)
```

time: 468 us -> 187 us (0.40)
  waiting for transfers between devices: 328 us -> 0 us
  Pallas kernels: 0 us -> 178 us
  other arithmetic: 73.7 us -> 0.76 us
  matrix products: 51.3 us -> 0 us
  starting transfers between devices: 9.11 us -> 0 us
    ppermute x5 -> x0, waiting for transfers between devices: 328 us -> none  [the longest x3 324 us: from_behind(): return lax.ppermute(value, axis, pairs)]
    pallas_call x0 -> x1, Pallas kernels: none -> 178 us  [shards(): pl.pallas_call(functools.partial(kernel, groups, bands), out_shape=jax.Sh...]
    dot_general x5 -> x0, matrix products: 51.3 us -> none  [the longest x3 49.9 us: correlate(): jnp.einsum('cspf,clsqf->plq', left_part, rotated, preferred_element_type=...]
    convert_element_type x3 -> x1, other arithmetic: 43.6 us -> 0.01 us  [shards(): inner.astype(F32)[None, :]]
    mul x5 -> x1, other arithmetic: 24.7 us -> 0.01 us  [shards(): math.pi * lag_values[:, None] * inner.astype(F32)[None, :] / (bands * bins)]
    ppermute x5 -> x0, starting transfers between devices: 9.11 us -> none  [the longest x1 4.87 us: padded_2(): lax.ppermute(tail, axis, [(i, (i + 1) % count) for i in range(ends)])]
    reshape x1, local copies, waits for them, and re-layouts: 0.34 us -> 6.53 us  [shards(): return jnp.transpose(out.reshape(ROUNDS, LAGS, chans, chans), (2, 0, 1, 3))]
    reduce_sum x2 -> x0, other arithmetic: 4.71 us -> none  [the longest x1 4.09 us: shards(): energy = jnp.sum(jnp.square(spectra.astype(jnp.float32)), axis=(0, 1))]
  transfers between devices with their start and end apart: 5 -> 0, of which waited for: 4 -> 0; matrix products, arithmetic and copies ran while one was open for 3% -> 0% of each run, Pallas kernels for 0% -> 0%
where the time goes in v1:
time: 187 us; the launch traced here: 185 us
  Pallas kernels  178 us (95%)
  local copies, waits for them, and re-layouts  6.53 us (3%)
    pallas_call x1, Pallas kernels, shards(): pl.pallas_call(functools.partial(kernel, groups, bands), out_shape=jax.Sh...  178 us
    reshape x1, local copies, waits for them, and re-layouts, shards(): return jnp.transpose(out.reshape(ROUNDS, LAGS, chans, chans), (2, 0, 1, 3))  6.53 us

profile of v1, /device:TPU:0, one launch (start us, length us, event | category | flops | bytes accessed | tf_op | source)
XLA Modules:
  0.0 184.9 jit_solution(8522213204070852242)
XLA Ops:
  0.0 0.7 fusion
  0.8 177.6 %shard_map.28 = bf16[3,1536,384]{2,1,0:T(8,128)(2,1)} custom-call(bf16[2,8,384,512]{3,2,1,0:T(8,128)(2,1)} %spectra.1, s32[1,512]{1,0:T(1,128)} %bitcast.6, f32[4,512]{1,0:T(4,128)} %get-tuple-element.6.cosines, f32[4,512]{1,0:T(4,128)} %get-tuple-element.5.sines), custom_call_target="tpu_custom_call" | custom-call | flops 28991029248 | bytes 25165824 | tf_op jit(solution)/shard_map/pallas_call | solution.py:254
  178.3 6.5 %copy.5 = bf16[3,4,384,384]{3,1,0,2:T(4,128)(2,1)} copy(bf16[3,4,384,384]{3,2,1,0:T(8,128)(2,1)} %bitcast.5) | data formatting | bytes 7077888 | tf_op jit(solution)/shard_map/reshape | solution.py:281
  (2 shorter events, 0.0 us)

commit v2 on v1

--- a/solution.py
+++ b/solution.py
@@ -100,9 +100,7 @@
     def _(s):
         load(s).start()
 
-    @pl.loop(0, EARLY)
-    def _(s):
-        start(own_flows, s)
+    start(own_flows, 0)
 
     @pl.loop(0, segs)
     def _(s):
@@ -117,6 +115,10 @@
                 part = rot[s, c, 0, rows, :].astype(F32)
                 total = total + part * part
         energy[rows, :] = total
+
+    @pl.loop(1, EARLY)
+    def _(s):
+        start(own_flows, s)
 
     member = (
         lax.broadcasted_iota(jnp.int32, (stations, chans), 1) // 3
@@ -166,6 +168,8 @@
     def _(s):
         start(own_flows, s)
 
+    forward(0)
+
     def expand(slot):
         scale[slot] = jnp.dot(
             spread, amps[slot], precision=HIGHEST, preferred_element_type=F32
@@ -192,7 +196,7 @@
                 rot[s, 1, lag, rows, :] = (imag * cosine - real * sine).astype(BF16)
 
     forward(segs)
-    forward(0)
+    forward(1)
     arrived(1, segs)
     start(swaps, segs)
     acc[...] = jnp.zeros_like(acc)
@@ -212,9 +216,9 @@
 
     @pl.loop(0, segs)
     def _(s):
-        @pl.when(s + 1 < segs)
+        @pl.when(s + 2 < segs)
         def _():
-            forward(s + 1)
+            forward(s + 2)
 
         arrived(1, s)
         start(swaps, s)

time: 187 us -> 178 us (0.952)
  Pallas kernels: 178 us -> 169 us
    pallas_call x1, Pallas kernels: 178 us -> 169 us  [shards(): pl.pallas_call(functools.partial(kernel, groups, bands), out_shape=jax.Sh...]
where the time goes in v2:
time: 178 us; the launch traced here: 176 us
  Pallas kernels  169 us (95%)
  local copies, waits for them, and re-layouts  6.53 us (4%)
    pallas_call x1, Pallas kernels, shards(): pl.pallas_call(functools.partial(kernel, groups, bands), out_shape=jax.Sh...  169 us
    reshape x1, local copies, waits for them, and re-layouts, shards(): return jnp.transpose(out.reshape(ROUNDS, LAGS, chans, chans), (2, 0, 1, 3))  6.53 us

profile of v2, /device:TPU:0, one launch (start us, length us, event | category | flops | bytes accessed | tf_op | source)
XLA Modules:
  0.0 176.4 jit_solution(6038702452072035480)
XLA Ops:
  0.0 0.7 fusion
  0.8 169.1 %shard_map.28 = bf16[3,1536,384]{2,1,0:T(8,128)(2,1)} custom-call(bf16[2,8,384,512]{3,2,1,0:T(8,128)(2,1)} %spectra.1, s32[1,512]{1,0:T(1,128)} %bitcast.6, f32[4,512]{1,0:T(4,128)} %get-tuple-element.6.cosines, f32[4,512]{1,0:T(4,128)} %get-tuple-element.5.sines), custom_call_target="tpu_custom_call" | custom-call | flops 28991029248 | bytes 25165824 | tf_op jit(solution)/shard_map/pallas_call | solution.py:258
  169.9 6.5 %copy.5 = bf16[3,4,384,384]{3,1,0,2:T(4,128)(2,1)} copy(bf16[3,4,384,384]{3,2,1,0:T(8,128)(2,1)} %bitcast.5) | data formatting | bytes 7077888 | tf_op jit(solution)/shard_map/reshape | solution.py:285
  (2 shorter events, 0.0 us)
